TPU v7x, 512 devices: a whole 4x4x16 slice. The times are simulated.
512 devices in a mesh: design: 16 (over y, x_lo, core), seq: 32 (over x_hi, z).
Axes of the slice: x: 4 (x_hi: 2, x_lo: 2; x = x_hi * 2 + x_lo), y: 4, z: 16, core: 2. Of those that a mesh axis runs over, the one named last changes fastest.
Arguments:
- window_x: bfloat16 [16, 512, 8192], P('design', 'seq'), may hold values from -6 to 6
- norm_gain: float32 [8192], replicated, may hold values from 0.5 to 1.5
- proj_weight: bfloat16 [8192, 3, 4096], P('design', None, 'seq'), may hold values from -0.0625 to 0.0625
- proj_tail: bfloat16 [16, 6, 3, 4096], P('design', None, None, 'seq'), may hold values from -6 to 6
- short_taps: float32 [7, 3, 4096], P(None, None, 'seq'), may hold values from -2 to 2
- decay_rates: float32 [4096, 16], replicated, may hold values from 8.680556e-06 to 0.035
- residues: float32 [4096, 16], P('seq'), may hold values from 0 to 0.03
- skip_bias: float32 [4096], P('seq'), may hold values from -6 to 6
- context_u: bfloat16 [16, 4096, 4096], P('design', 'seq'), may hold values from -6 to 6
- context_tokens: int32 [16, 4096], P('design', 'seq'), may hold values from 0 to 4, as said below
Outputs:
- mixed: bfloat16 [16, 512, 4096], P('design', None, 'seq')
Inputs may be any that keep to these rules, and one draw needn't show every extreme that they name: `context_tokens`: 0 marks padding and fills a prefix of 1 to 65 positions of each design's context; 1 to 4 are bases.
All inputs are finite; a program needn't handle non-finite values.
Results may differ from a plain program's by a relative error of at most 0.0059.
The roundings to bfloat16 on the way count: a program that leaves them out, or rounds other values in their place, can miss the bound.
Values may be sent and summed in bfloat16 or wider, within the bound.
No kernel may reach another device: no remote copies, remote signals or barrier semaphores. Data moves between devices by JAX's collectives and lax.ppermute only.
A program may use at most 128 MiB of HBM per device.

v0:
```python
import math
import jax
import jax.numpy as jnp
from jax import lax
from jax.sharding import PartitionSpec as P


def decayed_sum(values, distance, rate_table):
    columns = []
    for mode_index in range(rate_table.shape[1]):
        weights = jnp.exp(-rate_table[:, mode_index][None, :] * distance[:, None])
        columns.append(jnp.sum(values * weights, axis=0))
    return jnp.stack(columns, axis=1)


def dft_tables(length):
    indices = jnp.arange(length, dtype=jnp.int32)
    phase_int = indices[:, None] * indices[None, :] % length
    angles = phase_int.astype(jnp.float32) * (2.0 * math.pi / length)
    return (jnp.cos(angles), jnp.sin(angles))


def local(
    window_x,
    norm_gain,
    proj_weight,
    proj_tail,
    short_taps,
    decay_rates,
    residues,
    skip_bias,
    context_u,
    context_tokens,
):
    local_rows = window_x.shape[1]
    width = window_x.shape[2]
    local_chans = proj_weight.shape[2]
    seq_count = lax.axis_size("seq")
    window = local_rows * seq_count
    ctx_rows = context_u.shape[1]
    history = ctx_rows * seq_count
    seq_index = lax.axis_index("seq")
    highest = lax.Precision.HIGHEST
    rows_f = window_x[0].astype(jnp.float32)
    meansq = jnp.mean(rows_f * rows_f, axis=-1, keepdims=True)
    normed = (rows_f * lax.rsqrt(meansq + 1e-06) * norm_gain[None, :]).astype(jnp.bfloat16)
    weight_panel = lax.all_gather(proj_weight, "design", axis=0, tiled=True).reshape(
        width, 3 * local_chans
    )
    features = jnp.dot(
        lax.all_gather(normed, "seq", axis=0, tiled=True),
        weight_panel,
        preferred_element_type=jnp.float32,
    )
    features = features.astype(jnp.bfloat16).reshape(window, 3, local_chans)
    extended = jnp.concatenate([proj_tail[0], features], axis=0).astype(jnp.float32)
    filtered = jnp.zeros((window, 3, local_chans), jnp.float32)
    for tap_index in range(short_taps.shape[0]):
        begin_row = short_taps.shape[0] - 1 - tap_index
        filtered = filtered + short_taps[tap_index][None] * extended[begin_row : begin_row + window]
    queries = filtered[:, 0]
    inner_term = filtered[:, 1] * filtered[:, 2]
    rates_local = lax.dynamic_slice_in_dim(decay_rates, seq_index * local_chans, local_chans, 0)
    masked_hist = jnp.where(
        (context_tokens[0] != 0)[:, None], context_u[0], jnp.zeros((), jnp.bfloat16)
    )
    relaid = lax.all_to_all(masked_hist, "seq", split_axis=1, concat_axis=0, tiled=True)
    distance = (history - 1 - jnp.arange(history, dtype=jnp.int32)).astype(jnp.float32)
    states = decayed_sum(relaid.astype(jnp.float32), distance, rates_local)
    offsets = jnp.arange(window, dtype=jnp.int32).astype(jnp.float32)
    decay_grid = jnp.exp(-rates_local[None, :, :] * offsets[:, None, None])
    kernel = jnp.einsum("tcm,cm->tc", decay_grid, residues, precision=highest)
    carried = jnp.einsum(
        "tcm,cm->tc", decay_grid, residues * jnp.exp(-rates_local) * states, precision=highest
    )
    length = 2 * window
    cos_table, sin_table = dft_tables(length)
    zero_rows = jnp.zeros((window, local_chans), jnp.float32)

    def spectrum(values):
        padded = jnp.concatenate([values, zero_rows], axis=0)
        real_part = jnp.dot(cos_table, padded, precision=highest)
        imag_part = -jnp.dot(sin_table, padded, precision=highest)
        return (real_part, imag_part)

    inner_re, inner_im = spectrum(inner_term)
    kernel_re, kernel_im = spectrum(kernel)
    prod_re = inner_re * kernel_re - inner_im * kernel_im
    prod_im = inner_re * kernel_im + inner_im * kernel_re
    longconv = (
        jnp.dot(cos_table[:window], prod_re, precision=highest)
        - jnp.dot(sin_table[:window], prod_im, precision=highest)
    ) / length
    output_block = (queries * (longconv + carried + skip_bias[None, :] * inner_term)).astype(
        jnp.bfloat16
    )
    return output_block[None]


def solution(mesh):
    in_specs = (
        P("design", "seq", None),
        P(),
        P("design", None, "seq"),
        P("design", None, None, "seq"),
        P(None, None, "seq"),
        P(),
        P("seq", None),
        P("seq"),
        P("design", "seq", None),
        P("design", "seq"),
    )
    out_specs = P("design", None, "seq")
    return jax.shard_map(local, mesh=mesh, in_specs=in_specs, out_specs=out_specs, check_vma=False)
```

profile of v0, /device:TPU:32, one launch (start us, length us, event | category | flops | bytes accessed | tf_op | source)
XLA Modules:
  0.0 330.9 jit_solution(15777754056590807734)
XLA Ops:
  6.5 1.9 copy.29
  8.5 0.0 all-gather.5.cloned.1.call-update
  8.5 0.0 all-gather.3.cloned.1.call-start
  8.5 1.1 fusion.67
  9.7 1.8 fusion.69
  11.5 0.0 all-gather.3.cloned.1.call-update
  11.5 1.6 copy.31
  13.2 0.1 broadcast_select_fusion
  13.2 1.3 copy.32
  14.6 17.8 %all-to-all-start = ((bf16[128,32,128]{2,0,1:T(8,128)(2,1)}), bf16[128,32,128]{2,0,1:T(8,128)(2,1)S(1)}, u32[]{:S(2)}, u32[]{:S(2)}) async-start(bf16[128,32,128]{2,0,1:T(8,128)(2,1)} %copy.32), calls=%async_computation | async-start | bytes 2097152 | tf_op jit(solution)/shard_map/all_to_all | solution.py:67
  32.5 1.1 fusion.94
  33.7 16.2 %fusion.27 = f32[1024,1024]{1,0:T(8,128)} fusion(), kind=kLoop, calls=%fused_computation.49 | loop fusion | flops 14680064 | bytes 4194304 | tf_op jit(solution)/shard_map/cos | solution.py:20
  49.9 16.3 %fusion.26 = f32[1024,1024]{1,0:T(8,128)} fusion(), kind=kLoop, calls=%fused_computation.48 | loop fusion | flops 14680064 | bytes 4194304 | tf_op jit(solution)/shard_map/sin | solution.py:20
  66.2 22.2 %all-to-all-done = bf16[128,32,128]{2,0,1:T(8,128)(2,1)S(1)} async-done(((bf16[128,32,128]{2,0,1:T(8,128)(2,1)}), bf16[128,32,128]{2,0,1:T(8,128)(2,1)S(1)}, u32[]{:S(2)}, u32[]{:S(2)}) %all-to-all-start) | async-done | bytes 1048608 | tf_op jit(solution)/shard_map/all_to_all | solution.py:67
  88.4 5.9 %fusion.25 = (f32[128]{0:T(128)S(1)}, f32[128]{0:T(128)S(1)}, f32[128]{0:T(128)S(1)}, f32[128]{0:T(128)S(1)}, f32[128]{0:T(128)S(1)}, /*index=5*/f32[128]{0:T(12...) fusion(bf16[128,32,128]{2,0,1:T(8,128)(2,1)S(1)} %all-to-all-do, ...), kind=kLoop, calls=%fused_computation.47 | loop fusion | flops 25688064 | bytes 1081344 | tf_op jit(solution)/shard_map/reduce_sum | solution.py:12
  94.2 0.1 stack.67
  94.3 0.7 multiply_multiply_fusion
  95.0 3.1 multiply_reduce_fusion
  98.1 0.1 copy.38
  98.2 18.9 %fusion.32 = f32[1024,128]{1,0:T(8,128)S(1)} fusion(f32[512,128]{0,1:T(8,128)S(1)} %bitcast.143), kind=kOutput, calls=%fused_computation.52 | convolution fusion | flops 1625292800 | bytes 786432 | tf_op jit(solution)/shard_map/dot_general | solution.py:83
  117.2 19.2 %fusion.28 = f32[1024,128]{1,0:T(8,128)S(1)} fusion(f32[512,128]{0,1:T(8,128)S(1)} %bitcast.144), kind=kOutput, calls=%fused_computation.50 | convolution fusion | flops 1625292800 | bytes 786432 | tf_op jit(solution)/shard_map/dot_general | solution.py:82
  136.3 0.0 all-gather.5.cloned.1.call-done
  136.3 135.1 %all-gather.3.cloned.1.call-done = bf16[512,8192]{1,0:T(8,128)(2,1)} async-done(((bf16[16,8192]{1,0:T(8,128)(2,1)}), bf16[512,8192]{1,0:T(8,128)(2,1)}) %all-gather.3.cloned.1.call-update) | async-done | bytes 8388624 | tf_op jit(solution)/shard_map/all_gather | solution.py:51
  271.4 8.6 %convolution_convert_fusion = bf16[512,384]{0,1:T(8,128)(2,1)S(1)} fusion(bf16[512,8192]{1,0:T(8,128)(2,1)} %all-gather.3.cloned.1.call-done, bf16[8192,384]{0,1:T(8,128)(2,1)} %bitcast.163), kind=kOutput, calls=%fused_computation.54 | convolution fusion | flops 3221422080 | bytes 15073280 | tf_op jit(solution)/shard_map/dot_general | solution.py:50
  280.0 0.2 copy.30
  280.2 0.1 maximum_convert_fusion
  280.3 0.6 fusion.57
  281.0 19.4 %fusion.34 = f32[1024,128]{1,0:T(8,128)S(1)} fusion(f32[512,128]{1,0:T(8,128)S(1)} %fusion.78), kind=kOutput, calls=%fused_computation.53 | convolution fusion | flops 1625292800 | bytes 786432 | tf_op jit(solution)/shard_map/dot_general | solution.py:83
  300.4 18.8 %fusion.30 = f32[1024,128]{1,0:T(8,128)S(1)} fusion(f32[512,128]{1,0:T(8,128)S(1)} %fusion.78), kind=kOutput, calls=%fused_computation.51 | convolution fusion | flops 1625292800 | bytes 786432 | tf_op jit(solution)/shard_map/dot_general | solution.py:82
  319.2 1.8 fusion.6
  321.0 0.3 copy-done
  321.4 2.5 fusion.54
  (25 shorter events, 0.1 us)
Async XLA Ops:
  6.5 6.6 %copy-start.6 = (s32[1,128]{1,0:T(1,128)S(1)}, s32[1,128]{1,0:T(1,128)}, u32[]{:S(2)}) copy-start(s32[1,128]{1,0:T(1,128)} %param.19) | copy-start | bytes 1540
  6.5 129.8 %all-gather.5.cloned.1.call-start = ((), (), s32[]{:S(2)}) async-start(), calls=%async_computation.2 | async-start | bytes 6684672 | tf_op jit(solution)/shard_map/all_gather | solution.py:47
  8.5 262.9 %all-gather.3.cloned.1.call-start = ((), (), s32[]{:S(2)}) async-start(), calls=%async_computation.1 | async-start | bytes 8650752 | tf_op jit(solution)/shard_map/all_gather | solution.py:51
  11.5 20.9 %copy-start.4 = (bf16[1,6,3,128]{3,2,1,0:T(4,128)(2,1)S(1)}, bf16[1,6,3,128]{3,2,1,0:T(4,128)(2,1)}, u32[]{:S(2)}) copy-start(bf16[1,6,3,128]{3,2,1,0:T(4,128)(2,1)} %param.13) | copy-start | bytes 13828
  11.5 20.9 %copy-start.2 = (f32[7,3,128]{2,0,1:T(8,128)S(1)}, f32[7,3,128]{2,0,1:T(8,128)}, u32[]{:S(2)}) copy-start(f32[7,3,128]{2,0,1:T(8,128)} %param.14) | copy-start | bytes 32260
  14.6 73.8 %all-to-all-start = ((bf16[128,32,128]{2,0,1:T(8,128)(2,1)}), bf16[128,32,128]{2,0,1:T(8,128)(2,1)S(1)}, u32[]{:S(2)}, u32[]{:S(2)}) async-start(bf16[128,32,128]{2,0,1:T(8,128)(2,1)} %copy.32), calls=%async_computation | async-start | bytes 2097152 | tf_op jit(solution)/shard_map/all_to_all | solution.py:67
  88.4 5.9 %copy-start.3 = (f32[128,16]{0,1:T(8,128)S(1)}, f32[128,16]{0,1:T(8,128)}, u32[]{:S(2)}) copy-start(f32[128,16]{0,1:T(8,128)} %param.16) | copy-start | bytes 24580
  300.4 18.8 %copy-start.1 = (f32[1024,1024]{1,0:T(8,128)S(1)}, f32[1024,1024]{1,0:T(8,128)}, u32[]{:S(2)}) copy-start(f32[1024,1024]{1,0:T(8,128)} %fusion.26) | copy-start | bytes 12582916
  319.2 2.2 copy-start
  319.2 2.2 copy-start.5
Sparse Core Ops, SparseCore 0:
  9.5 62.8 all-gather.4
  75.4 195.9 all-gather.2
where the time goes:
time: 337 us; the launch traced here: 331 us
  waiting for transfers between devices  157 us (47%)
  matrix products  89.1 us (26%)
  other arithmetic  47.1 us (14%)
  starting transfers between devices  17.9 us (5%)
  between operations  13.9 us (4%)
  local copies, waits for them, and re-layouts  5.67 us (2%)
    all_gather x1, waiting for transfers between devices, local(): lax.all_gather(normed, 'seq', axis=0, tiled=True)  135 us
    dot_general x2, matrix products, spectrum(): imag_part = -jnp.dot(sin_table, padded, precision=highest)  38.3 us
    dot_general x2, matrix products, spectrum(): real_part = jnp.dot(cos_table, padded, precision=highest)  37.9 us
    all_to_all x1, waiting for transfers between devices, local(): lax.all_to_all(masked_hist, 'seq', split_axis=1, concat_axis=0, tiled=True)  22.2 us
    all_to_all x1, starting transfers between devices, local(): lax.all_to_all(masked_hist, 'seq', split_axis=1, concat_axis=0, tiled=True)  17.8 us
    sin x1, other arithmetic, dft_tables(): return (jnp.cos(angles), jnp.sin(angles))  16.3 us
    cos x1, other arithmetic, dft_tables(): return (jnp.cos(angles), jnp.sin(angles))  16.2 us
    dot_general x1, matrix products, local(): jnp.dot(lax.all_gather(normed, 'seq', axis=0, tiled=True), weight_panel,...  8.6 us
  transfers between devices with their start and end apart: 3, of which 2 were waited for; matrix products, arithmetic and copies ran while one was open for 26% of the time, Pallas kernels for 0%

commit v1 on v0

--- a/solution.py
+++ b/solution.py
@@ -47,11 +47,10 @@
     weight_panel = lax.all_gather(proj_weight, "design", axis=0, tiled=True).reshape(
         width, 3 * local_chans
     )
-    features = jnp.dot(
-        lax.all_gather(normed, "seq", axis=0, tiled=True),
-        weight_panel,
-        preferred_element_type=jnp.float32,
+    set_page = lambda link_axis, local_x: jnp.concatenate(
+        lax.all_to_all(jnp.stack(lax.axis_size(link_axis) * [local_x], 0), link_axis, 0, 0), 0
     )
+    features = jnp.dot(set_page("seq", normed), weight_panel, preferred_element_type=jnp.float32)
     features = features.astype(jnp.bfloat16).reshape(window, 3, local_chans)
     extended = jnp.concatenate([proj_tail[0], features], axis=0).astype(jnp.float32)
     filtered = jnp.zeros((window, 3, local_chans), jnp.float32)

time: 337 us -> 529 us (1.57)
  the two profiles are of different devices: /device:TPU:32 before, /device:TPU:120 now
where the time goes in v1:
time: 529 us; the launch traced here: 522 us
  waiting for transfers between devices  342 us (65%)
  matrix products  89.1 us (17%)
  other arithmetic  45.2 us (9%)
  starting transfers between devices  23.5 us (4%)
  between operations  13.9 us (3%)
  local copies, waits for them, and re-layouts  8.99 us (2%)
    all_to_all x1, waiting for transfers between devices, local(): lax.all_to_all(jnp.stack(lax.axis_size(link_axis) * [local_x], 0), link_a...  288 us
    all_to_all x1, waiting for transfers between devices, local(): lax.all_to_all(masked_hist, 'seq', split_axis=1, concat_axis=0, tiled=True)  53.6 us
    dot_general x2, matrix products, spectrum(): imag_part = -jnp.dot(sin_table, padded, precision=highest)  38.1 us
    dot_general x2, matrix products, spectrum(): real_part = jnp.dot(cos_table, padded, precision=highest)  38.1 us
    all_to_all x1, starting transfers between devices, local(): lax.all_to_all(masked_hist, 'seq', split_axis=1, concat_axis=0, tiled=True)  16.9 us
    sin x1, other arithmetic, dft_tables(): return (jnp.cos(angles), jnp.sin(angles))  16.3 us
    cos x1, other arithmetic, dft_tables(): return (jnp.cos(angles), jnp.sin(angles))  16.2 us
  transfers between devices with their start and end apart: 3, of which 2 were waited for; matrix products, arithmetic and copies ran while one was open for 16% of the time, Pallas kernels for 0%

profile of v1, /device:TPU:120, one launch (start us, length us, event | category | flops | bytes accessed | tf_op | source)
XLA Modules:
  0.0 522.3 jit_solution(7101642024298922101)
XLA Ops:
  6.5 1.7 copy.31
  8.2 0.7 compare_bitcast_fusion
  8.9 0.1 broadcast_select_fusion
  8.9 1.3 copy.32
  10.3 16.9 %all-to-all-start.1 = ((bf16[128,32,128]{2,0,1:T(8,128)(2,1)}), bf16[128,32,128]{2,0,1:T(8,128)(2,1)S(1)}, u32[]{:S(2)}, u32[]{:S(2)}) async-start(bf16[128,32,128]{2,0,1:T(8,128)(2,1)} %copy.32), calls=%async_computation.1 | async-start | bytes 2097152 | tf_op jit(solution)/shard_map/all_to_all | solution.py:66
  27.2 0.2 fusion.67
  27.4 0.1 fusion.78
  27.5 53.6 %all-to-all-done.1 = bf16[128,32,128]{2,0,1:T(8,128)(2,1)S(1)} async-done(((bf16[128,32,128]{2,0,1:T(8,128)(2,1)}), bf16[128,32,128]{2,0,1:T(8,128)(2,1)S(1)}, u32[]{:S(2)}, u32[]{:S(2)}) %all-to-all-start.1) | async-done | bytes 1048608 | tf_op jit(solution)/shard_map/all_to_all | solution.py:66
  81.2 4.2 stack.39
  85.4 6.6 %all-to-all-start = ((bf16[32,16,8192]{2,1,0:T(8,128)(2,1)}), bf16[32,16,8192]{2,1,0:T(8,128)(2,1)}, u32[]{:S(2)}, u32[]{:S(2)}) async-start(bf16[32,16,8192]{2,1,0:T(8,128)(2,1)} %stack.39), calls=%async_computation | async-start | bytes 16777216 | tf_op jit(solution)/shard_map/all_to_all | solution.py:51
  92.0 0.0 all-gather.2.cloned.1.call-start
  92.0 1.0 copy.29
  93.1 1.1 fusion.95
  94.3 16.3 %fusion.26 = f32[1024,1024]{1,0:T(8,128)} fusion(), kind=kLoop, calls=%fused_computation.48 | loop fusion | flops 14680064 | bytes 4194304 | tf_op jit(solution)/shard_map/sin | solution.py:20
  110.6 16.2 %fusion.27 = f32[1024,1024]{1,0:T(8,128)} fusion(), kind=kLoop, calls=%fused_computation.49 | loop fusion | flops 14680064 | bytes 4194304 | tf_op jit(solution)/shard_map/cos | solution.py:20
  126.9 5.9 %fusion.25 = (f32[128]{0:T(128)S(1)}, f32[128]{0:T(128)S(1)}, f32[128]{0:T(128)S(1)}, f32[128]{0:T(128)S(1)}, f32[128]{0:T(128)S(1)}, /*index=5*/f32[128]{0:T(12...) fusion(bf16[128,32,128]{2,0,1:T(8,128)(2,1)S(1)} %all-to-all-do, ...), kind=kLoop, calls=%fused_computation.47 | loop fusion | flops 25688064 | bytes 1081344 | tf_op jit(solution)/shard_map/reduce_sum | solution.py:12
  132.7 0.1 stack.106
  132.8 0.7 multiply_multiply_fusion
  133.5 3.1 multiply_reduce_fusion
  136.6 0.1 copy.38
  136.8 18.8 %fusion.28 = f32[1024,128]{1,0:T(8,128)S(1)} fusion(f32[512,128]{0,1:T(8,128)S(1)} %bitcast.142), kind=kOutput, calls=%fused_computation.50 | convolution fusion | flops 1625292800 | bytes 786432 | tf_op jit(solution)/shard_map/dot_general | solution.py:81
  155.6 19.3 %fusion.32 = f32[1024,128]{1,0:T(8,128)S(1)} fusion(f32[512,128]{0,1:T(8,128)S(1)} %bitcast.143), kind=kOutput, calls=%fused_computation.52 | convolution fusion | flops 1625292800 | bytes 786432 | tf_op jit(solution)/shard_map/dot_general | solution.py:82
  174.9 287.9 %all-to-all-done = bf16[32,16,8192]{2,1,0:T(8,128)(2,1)} async-done(((bf16[32,16,8192]{2,1,0:T(8,128)(2,1)}), bf16[32,16,8192]{2,1,0:T(8,128)(2,1)}, u32[]{:S(2)}, u32[]{:S(2)}) %all-to-all-start) | async-done | bytes 8388640 | tf_op jit(solution)/shard_map/all_to_all | solution.py:51
  462.8 8.6 %convolution_convert_fusion = bf16[512,384]{0,1:T(8,128)(2,1)S(1)} fusion(bf16[512,8192]{1,0:T(8,128)(2,1)} %bitcast.4, bf16[8192,384]{0,1:T(8,128)(2,1)} %bitcast.162), kind=kOutput, calls=%fused_computation.54 | convolution fusion | flops 3221422080 | bytes 15073280 | tf_op jit(solution)/shard_map/dot_general | solution.py:53
  471.4 0.2 copy.30
  471.7 0.1 maximum_convert_fusion
  471.8 0.6 fusion.57
  472.4 19.3 %fusion.30 = f32[1024,128]{1,0:T(8,128)S(1)} fusion(f32[512,128]{1,0:T(8,128)S(1)} %fusion.79), kind=kOutput, calls=%fused_computation.51 | convolution fusion | flops 1625292800 | bytes 786432 | tf_op jit(solution)/shard_map/dot_general | solution.py:81
  491.7 18.9 %fusion.34 = f32[1024,128]{1,0:T(8,128)S(1)} fusion(f32[512,128]{1,0:T(8,128)S(1)} %fusion.79), kind=kOutput, calls=%fused_computation.53 | convolution fusion | flops 1625292800 | bytes 786432 | tf_op jit(solution)/shard_map/dot_general | solution.py:82
  510.6 1.8 fusion.6
  512.4 0.3 copy-done
  512.8 2.5 fusion.54
  (29 shorter events, 0.2 us)
Async XLA Ops:
  6.5 20.6 %copy-start.2 = (bf16[1,16,8192]{2,1,0:T(8,128)(2,1)S(1)}, bf16[1,16,8192]{2,1,0:T(8,128)(2,1)}, u32[]{:S(2)}) copy-start(bf16[1,16,8192]{2,1,0:T(8,128)(2,1)} %param.10) | copy-start | bytes 786436
  6.5 20.9 %copy-start.4 = (f32[8192]{0:T(1024)S(1)}, f32[8192]{0:T(1024)}, u32[]{:S(2)}) copy-start(f32[8192]{0:T(1024)} %param.11) | copy-start | bytes 98308
  10.3 70.9 %all-to-all-start.1 = ((bf16[128,32,128]{2,0,1:T(8,128)(2,1)}), bf16[128,32,128]{2,0,1:T(8,128)(2,1)S(1)}, u32[]{:S(2)}, u32[]{:S(2)}) async-start(bf16[128,32,128]{2,0,1:T(8,128)(2,1)} %copy.32), calls=%async_computation.1 | async-start | bytes 2097152 | tf_op jit(solution)/shard_map/all_to_all | solution.py:66
  85.4 6.7 %copy-start.3 = (bf16[512,3,128]{2,0,1:T(8,128)(2,1)S(1)}, bf16[512,3,128]{2,0,1:T(8,128)(2,1)}, u32[]{:S(2)}) copy-start(bf16[512,3,128]{2,0,1:T(8,128)(2,1)} %param.12) | copy-start | bytes 1179652
  85.4 7.7 %copy-start.5 = (f32[7,3,128]{2,0,1:T(8,128)S(1)}, f32[7,3,128]{2,0,1:T(8,128)}, u32[]{:S(2)}) copy-start(f32[7,3,128]{2,0,1:T(8,128)} %param.14) | copy-start | bytes 32260
  85.4 7.7 %copy-start.7 = (bf16[1,6,3,128]{3,2,1,0:T(4,128)(2,1)S(1)}, bf16[1,6,3,128]{3,2,1,0:T(4,128)(2,1)}, u32[]{:S(2)}) copy-start(bf16[1,6,3,128]{3,2,1,0:T(4,128)(2,1)} %param.13) | copy-start | bytes 13828
  85.4 377.4 %all-to-all-start = ((bf16[32,16,8192]{2,1,0:T(8,128)(2,1)}), bf16[32,16,8192]{2,1,0:T(8,128)(2,1)}, u32[]{:S(2)}, u32[]{:S(2)}) async-start(bf16[32,16,8192]{2,1,0:T(8,128)(2,1)} %stack.39), calls=%async_computation | async-start | bytes 16777216 | tf_op jit(solution)/shard_map/all_to_all | solution.py:51
  92.0 82.9 %all-gather.2.cloned.1.call-start = ((), (), s32[]{:S(2)}) async-start(), calls=%async_computation.2 | async-start | bytes 6684672 | tf_op jit(solution)/shard_map/all_gather | solution.py:47
  126.9 5.9 %copy-start.6 = (f32[128,16]{0,1:T(8,128)S(1)}, f32[128,16]{0,1:T(8,128)}, u32[]{:S(2)}) copy-start(f32[128,16]{0,1:T(8,128)} %param.16) | copy-start | bytes 24580
  491.7 18.9 %copy-start.1 = (f32[1024,1024]{1,0:T(8,128)S(1)}, f32[1024,1024]{1,0:T(8,128)}, u32[]{:S(2)}) copy-start(f32[1024,1024]{1,0:T(8,128)} %fusion.26) | copy-start | bytes 12582916
  510.6 2.2 copy-start
  510.6 2.2 copy-start.8
Sparse Core Ops, SparseCore 0:
  94.9 62.0 all-gather.1
